TPU v7x, 768 devices: a whole 4x8x12 slice. The times are simulated.
768 devices in a mesh: seq: 48 (over z, x), tp: 16 (over y, core).
Axes of the slice: x: 4, y: 8, z: 12, core: 2. Of those that a mesh axis runs over, the one named last changes fastest.
Arguments:
- hidden: bfloat16 [49152, 3584], P('seq', 'tp'), may hold values from -6 to 6
- grad_out: bfloat16 [49152, 3584], P('seq', 'tp'), may hold values from -24 to 24
- router_w: float32 [3584], replicated, may hold values from -0.09375 to 0.09375
- norm_gain: bfloat16 [3584], replicated, may hold values from 0.099609375 to 1.8984375
- gate_w: bfloat16 [3584, 7168], P(None, 'tp'), may hold values from -0.09375 to 0.09375
- up_w: bfloat16 [3584, 7168], P(None, 'tp'), may hold values from -0.09375 to 0.09375
- down_w: bfloat16 [7168, 3584], P('tp'), may hold values from -0.0625 to 0.0625
- counts: int32 [48], P('seq'), may hold values from 1 to 384, 6144 in all
- order: int32 [48, 1024], P('seq'), may hold values from 0 to 1023, each once within a row
Outputs:
- unit_scores: float32 [3, 7168], P(None, 'tp')
- router_score: float32 [3584], P('tp')
Inputs may be any that keep to these rules, and one draw needn't show every extreme that they name: The counts sum to 6144; the largest is exactly 384. `order`: each row is a permutation of the shard's local token indices.
All inputs are finite; a program needn't handle non-finite values. No bound on the sum of `counts` on one device may be relied on, other than what follows from the above.
Results may differ from a plain program's by a relative error of at most 0.0043.
Values may be sent and summed in bfloat16 or wider, within the bound.
A program may use at most 64 MiB of HBM per device.

v0:
```python
import jax
import jax.numpy as jnp
from jax import lax
from jax.sharding import PartitionSpec as P

D = 3584


epsilon = 1e-06


def gelu_pair(gate_proj):
    activation, pullback = jax.vjp(lambda inputs: jax.nn.gelu(inputs, approximate=True), gate_proj)
    slope = pullback(jnp.ones_like(gate_proj))[0]
    return (activation, slope)


def body(hidden, grad_out, router_w, norm_gain, gate_w, up_w, down_w, counts, order):
    shards = lax.axis_size("seq")
    tok_dev = hidden.shape[0]
    local_width = hidden.shape[1]
    average = tok_dev // 8
    slot_count = 3 * average
    picked = order[0, :slot_count]
    live_rows = jnp.arange(slot_count, dtype=jnp.int32) < counts[0]
    nothing = jnp.zeros((), jnp.bfloat16)
    feature_rows = jnp.where(live_rows[:, None], hidden[picked], nothing)
    cotangent_rows = jnp.where(live_rows[:, None], grad_out[picked], nothing)
    gain_f32 = norm_gain.astype(jnp.float32)
    feature_piece = lax.all_gather(feature_rows, "tp", axis=1, tiled=True)
    cotangent_piece = lax.all_gather(cotangent_rows, "tp", axis=1, tiled=True)
    piece_f32 = feature_piece.astype(jnp.float32)
    scaled = (piece_f32 * gain_f32).astype(jnp.bfloat16)
    gate_sum = jnp.dot(scaled, gate_w, preferred_element_type=jnp.float32)
    up_sum = jnp.dot(scaled, up_w, preferred_element_type=jnp.float32)
    back_sum = lax.dot_general(
        cotangent_piece, down_w, (((1,), (1,)), ((), ())), preferred_element_type=jnp.float32
    )
    square_sum = jnp.sum(piece_f32 * piece_f32, axis=1)
    logit_sum = jnp.sum(piece_f32 * router_w, axis=1)
    gate_raw, up_raw, back_proj, square_sum, logits = (
        gate_sum,
        up_sum,
        back_sum,
        square_sum,
        logit_sum,
    )
    inverse_rms = lax.rsqrt(square_sum / D + epsilon)
    gate_proj = gate_raw * inverse_rms[:, None]
    up_proj = up_raw * inverse_rms[:, None]
    router_prob = jax.nn.sigmoid(logits)
    activation, slope = gelu_pair(gate_proj)
    hidden_units = activation * up_proj
    grad_hidden = router_prob[:, None] * back_proj
    unit_terms = jnp.stack(
        [
            jnp.sum(gate_proj * grad_hidden * up_proj * slope, axis=0),
            jnp.sum(up_proj * grad_hidden * activation, axis=0),
            jnp.sum(hidden_units * grad_hidden, axis=0),
        ]
    )
    partial_dot = jnp.sum(hidden_units * back_proj, axis=1)
    full_dot = lax.psum(partial_dot, "tp")
    router_coef = router_prob * (1.0 - router_prob) * full_dot
    router_terms = jnp.sum(router_coef[:, None] * feature_rows.astype(jnp.float32), axis=0)
    unit_total, router_total = lax.psum((unit_terms, router_terms), "seq")
    router_local = lax.dynamic_slice_in_dim(
        router_w, lax.axis_index("tp") * local_width, local_width
    )
    factor = float(average * shards) ** (-0.5)
    return (unit_total * factor, router_local * router_total * factor)


def solution(mesh):
    in_specs = (
        P("seq", "tp"),
        P("seq", "tp"),
        P(),
        P(),
        P(None, "tp"),
        P(None, "tp"),
        P("tp", None),
        P("seq"),
        P("seq", None),
    )
    out_specs = (P(None, "tp"), P("tp"))
    return jax.shard_map(body, mesh=mesh, in_specs=in_specs, out_specs=out_specs, check_vma=False)
```

profile of v0, /device:TPU:32, one launch (start us, length us, event | category | flops | bytes accessed | tf_op | source)
XLA Modules:
  0.0 275.3 jit_solution(1195180870339273778)
XLA Ops:
  7.2 0.0 copy-start
  7.2 0.0 all-gather.3.cloned.1.call-start
  8.0 0.8 fusion.15
  8.9 2.0 copy.15
  10.9 0.0 copy-start.3
  10.9 0.0 copy-start.2
  10.9 2.0 copy.17
  12.9 3.3 %gather_fusion = bf16[384,224]{1,0:T(8,128)(2,1)} fusion(bf16[1024,224]{1,0:T(8,128)(2,1)} %copy.15, s32[1024]{0:T(1024)S(1)} %pad_clamp_fusion), kind=kCustom, calls=%fused_computation | custom fusion | bytes 345600 | tf_op jit(solution)/shard_map/gather | solution.py:27
  16.2 3.3 %gather_fusion.1 = bf16[384,224]{1,0:T(8,128)(2,1)} fusion(bf16[1024,224]{1,0:T(8,128)(2,1)} %copy.17, s32[1024]{0:T(1024)S(1)} %pad_clamp_fusion), kind=kCustom, calls=%fused_computation.1 | custom fusion | bytes 345600 | tf_op jit(solution)/shard_map/gather | solution.py:28
  19.5 1.8 broadcast_select_fusion
  21.3 0.8 copy.16
  22.1 0.0 all-gather.3.cloned.1.call-update
  22.1 0.0 all-gather.5.cloned.1.call-start
  22.2 1.7 copy.18
  23.9 0.0 all-gather.5.cloned.1.call-update
  23.9 0.0 copy-done.3
  24.0 48.1 %all-gather.3.cloned.1.call-done = bf16[384,3584]{0,1:T(8,128)(2,1)} async-done(((bf16[384,224]{0,1:T(8,128)(2,1)}), bf16[384,3584]{0,1:T(8,128)(2,1)}) %all-gather.3.cloned.1.call-update) | async-done | bytes 2752528 | tf_op jit(solution)/shard_map/all_gather | solution.py:30
  72.0 0.0 copy-done.2
  72.0 2.9 %fusion.1 = (f32[384]{0:T(512)S(1)}, f32[384]{0:T(512)S(1)}) fusion(bf16[384,3584]{0,1:T(8,128)(2,1)} %all-gather.3.cloned.1.call-done, f32[3584]{0:T(1024)S(1)} %copy-done.2), kind=kLoop, calls=%fused_computation.6 | loop fusion | flops 6880512 | bytes 2769920 | tf_op jit(solution)/shard_map/reduce_sum | solution.py:39
  75.0 44.1 %all-gather.5.cloned.1.call-done = bf16[384,3584]{0,1:T(8,128)(2,1)} async-done(((bf16[384,224]{0,1:T(8,128)(2,1)}), bf16[384,3584]{0,1:T(8,128)(2,1)}) %all-gather.5.cloned.1.call-update) | async-done | bytes 2752528 | tf_op jit(solution)/shard_map/all_gather | solution.py:31
  119.1 0.0 copy-done
  119.1 0.0 copy-start.1
  119.1 0.0 copy-start.4
  119.1 3.7 %fusion.16 = f32[384,448]{0,1:T(8,128)S(1)} fusion(bf16[448,3584]{1,0:T(8,128)(2,1)S(1)} %copy-done, bf16[384,3584]{0,1:T(8,128)(2,1)} %all-gather.5.cloned.1.call-done), kind=kOutput, calls=%fused_computation.39 | convolution fusion | flops 1233125376 | bytes 6651904 | tf_op jit(solution)/shard_map/dot_general | solution.py:36
  122.8 0.0 copy-done.1
  122.8 0.0 copy-done.4
  122.9 0.0 copy-start.5
  122.9 1.9 convolution_multiply_fusion
  124.8 0.0 copy-done.5
  124.8 2.7 fusion.12
  127.5 25.9 %psum.22 = f32[384]{0:T(512)S(1)} all-reduce(f32[384]{0:T(512)S(1)} %get-tuple-element.7), channel_id=1, replica_groups=mesh['seq'=48,'tp'=16] {'tp'}, use_global_device_ids=true, to_apply=%region_7.8 | all-reduce | flops 384 | bytes 3072 | tf_op jit(solution)/shard_map/psum | solution.py:63
  153.5 0.1 multiply_reduce_fusion.3
  153.6 113.6 %all-reduce = (f32[3,448]{1,0:T(4,128)S(1)}, f32[224]{0:T(256)S(1)}) all-reduce(f32[3,448]{1,0:T(4,128)S(1)} %pad_maximum_fusion, f32[224]{0:T(256)S(1)} %multiply_reduce_fusion.3), channel_id=1, replica_groups=mesh['seq'=48,'tp'=16] {'seq'}, use_global_device_ids=true, to_apply=%region_5.6 | all-reduce | flops 1568 | bytes 12544 | tf_op jit(solution)/shard_map/psum | solution.py:66
  267.2 0.6 broadcast_multiply_fusion
  267.8 0.6 multiply_multiply_fusion.3
  (6 shorter events, 0.1 us)
Async XLA Ops:
  7.2 111.9 %copy-start = (bf16[448,3584]{1,0:T(8,128)(2,1)S(1)}, bf16[448,3584]{1,0:T(8,128)(2,1)}, u32[]{:S(2)}) copy-start(bf16[448,3584]{1,0:T(8,128)(2,1)} %param.15) | copy-start | bytes 9633796
  7.2 64.8 %all-gather.3.cloned.1.call-start = ((), (), s32[]{:S(2)}) async-start(), calls=%async_computation | async-start | bytes 2924544 | tf_op jit(solution)/shard_map/all_gather | solution.py:30
  10.9 13.0 %copy-start.3 = (bf16[3584]{0:T(1024)(128)(2,1)S(1)}, bf16[3584]{0:T(1024)(128)(2,1)}, u32[]{:S(2)}) copy-start(bf16[3584]{0:T(1024)(128)(2,1)} %param.12) | copy-start | bytes 21508
  10.9 61.1 %copy-start.2 = (f32[3584]{0:T(1024)S(1)}, f32[3584]{0:T(1024)}, u32[]{:S(2)}) copy-start(f32[3584]{0:T(1024)} %param.11) | copy-start | bytes 43012
  22.1 97.0 %all-gather.5.cloned.1.call-start = ((), (), s32[]{:S(2)}) async-start(), calls=%async_computation.1 | async-start | bytes 2924544 | tf_op jit(solution)/shard_map/all_gather | solution.py:31
  119.1 3.7 %copy-start.1 = (bf16[384,3584]{0,1:T(8,128)(2,1)S(1)}, bf16[384,3584]{0,1:T(8,128)(2,1)}, u32[]{:S(2)}) copy-start(bf16[384,3584]{0,1:T(8,128)(2,1)} %all-gather.3.cloned.1.call-done) | copy-start | bytes 8257540
  119.1 3.8 %copy-start.4 = (bf16[3584,448]{0,1:T(8,128)(2,1)S(1)}, bf16[3584,448]{0,1:T(8,128)(2,1)}, u32[]{:S(2)}) copy-start(bf16[3584,448]{0,1:T(8,128)(2,1)} %param.14) | copy-start | bytes 9633796
  122.9 1.9 copy-start.5
Sparse Core Ops, SparseCore 0:
  22.2 49.7 all-gather.2
  74.4 44.6 all-gather.4
where the time goes:
time: 276 us; the launch traced here: 275 us
  blocking collectives  140 us (51%)
  waiting for transfers between devices  92.2 us (33%)
  between operations  14.9 us (5%)
  local copies, waits for them, and re-layouts  13.2 us (5%)
  matrix products  8.34 us (3%)
  other arithmetic  7.01 us (3%)
    psum x1, blocking collectives, body(): unit_total, router_total = lax.psum((unit_terms, router_terms), 'seq')  114 us
    all_gather x1, waiting for transfers between devices, body(): feature_piece = lax.all_gather(feature_rows, 'tp', axis=1, tiled=True)  48.1 us
    all_gather x1, waiting for transfers between devices, body(): cotangent_piece = lax.all_gather(cotangent_rows, 'tp', axis=1, tiled=True)  44.1 us
    psum x1, blocking collectives, body(): full_dot = lax.psum(partial_dot, 'tp')  25.9 us
  transfers between devices with their start and end apart: 2, of which 2 were waited for; matrix products, arithmetic and copies ran while one was open for 2% of the time, Pallas kernels for 0%

commit v1 on v0

v1 whole, which is shorter than its diff:
```python
import functools

import jax
import jax.numpy as jnp
from jax import lax
from jax.experimental import pallas as pl
from jax.experimental.pallas import tpu as pltpu
from jax.sharding import PartitionSpec as P

MESH = pl.DeviceIdType.MESH
LANES = 128
CORES = 2
X_CHIPS = 4
EPSILON = 1e-06
ROOT = 0.7978845608028654
CUBIC = 0.044715


def column(row):
    return jnp.transpose(jnp.broadcast_to(row, (LANES, LANES)))


def kernel(
    sizes,
    hidden_hbm, grad_hbm, router_hbm, gain_hbm, gate_hbm, up_hbm, down_hbm, counts_ref, order_hbm,
    unit_ref, score_ref,
    hidden_v, grad_v, gate_v, up_v, down_v, router_v, gain_v, order_v, held, gain_col, router_col,
    gate_sum, up_sum, back_sum, unit_sum, dots, unit_x, unit_z, score_x, score_z,
    load_sem, near_sem, ring_send, ring_recv, dot_send, dot_recv, ux_send, ux_recv, uz_send, uz_recv,
    sx_send, sx_recv, sz_send, sz_recv,
):
    xs, zs, ys, chunks, factor = sizes
    tp = ys * CORES
    width = hidden_v.shape[0]
    tokens = hidden_v.shape[1]
    features = width * tp
    seq_me = lax.axis_index("seq")
    tp_me = lax.axis_index("tp")
    x_me, z_me = lax.rem(seq_me, xs), seq_me // xs
    y_me, core = tp_me // CORES, lax.rem(tp_me, CORES)
    sibling = y_me * CORES + (1 - core)

    def block_at(distance, of_core):
        return lax.rem(y_me + distance + ys, ys) * CORES + of_core

    right, left = block_at(1, core), block_at(-1, core)

    loads = [
        pltpu.make_async_copy(source, target, load_sem.at[i])
        for i, (source, target) in enumerate(
            [
                (order_hbm, order_v), (hidden_hbm, hidden_v), (grad_hbm, grad_v),
                (router_hbm, router_v), (gain_hbm, gain_v), (gate_hbm, gate_v), (up_hbm, up_v), (down_hbm, down_v),
            ]
        )
    ]
    for load in loads:
        load.start()

    barrier = pltpu.get_barrier_semaphore()
    along_x = lambda i: z_me * xs + lax.rem(i + xs, xs)
    along_z = lambda i: lax.rem(i + zs, zs) * xs + x_me
    beside_x = [along_x(x_me + i) for i in ((1, -1) if xs > 2 else (1,) if xs > 1 else ())]
    beside_z = [along_z(z_me + i) for i in ((1, -1) if zs > 2 else (1,) if zs > 1 else ())]
    beside_y = [right, left] if ys > 2 else [right]
    for peer in beside_y + [sibling]:
        pl.semaphore_signal(barrier, inc=1, device_id={"tp": peer}, device_id_type=MESH)
    for peer in beside_x + beside_z:
        pl.semaphore_signal(barrier, inc=1, device_id={"seq": peer}, device_id_type=MESH)

    rounds = max(zs // 2, xs // 2) - 1

    def relay(i):
        if not 0 <= i < rounds:
            return
        peers = (beside_x if i + 1 < xs // 2 else []) + (beside_z if i + 1 < zs // 2 else [])
        if i > 0:
            relay_wait(i - 1)
        for peer in peers:
            pl.semaphore_signal(near_sem.at[i], inc=1, device_id={"seq": peer}, device_id_type=MESH)

    def relay_wait(i):
        peers = (beside_x if i + 1 < xs // 2 else []) + (beside_z if i + 1 < zs // 2 else [])
        if peers:
            pl.semaphore_wait(near_sem.at[i], len(peers))

    token = lax.broadcasted_iota(jnp.int32, (tokens, LANES), 0)
    slot = lax.broadcasted_iota(jnp.int32, (1, LANES), 1)
    loads[0].wait()
    count = counts_ref[0]

    def select(chunk):
        wanted = order_v[:, chunk * LANES : (chunk + 1) * LANES]
        wanted = jnp.where(slot + chunk * LANES < count, wanted, -1)
        chosen = jnp.where(token == wanted, 1.0, 0.0).astype(jnp.bfloat16)
        if chunk == 0:
            loads[1].wait()
        rows = jnp.dot(hidden_v[...], chosen, preferred_element_type=jnp.float32)
        held[chunk, 0, tp_me] = rows.astype(jnp.bfloat16)
        if chunk == 0:
            loads[2].wait()
        rows = jnp.dot(grad_v[...], chosen, preferred_element_type=jnp.float32)
        held[chunk, 1, tp_me] = rows.astype(jnp.bfloat16)

    select(0)
    pl.semaphore_wait(barrier, len(beside_y) + 1 + len(beside_x) + len(beside_z))

    sent = []

    def pass_on(chunk, array, block, way):
        target = (right, left, sibling)[way]
        copy = pltpu.make_async_remote_copy(
            src_ref=held.at[chunk, array, block],
            dst_ref=held.at[chunk, array, block],
            send_sem=ring_send.at[chunk, array, block, way],
            recv_sem=ring_recv.at[chunk, array, block],
            device_id={"tp": target},
            device_id_type=MESH,
        )
        copy.start()
        sent.append(copy)

    def arrive(chunk, array, block):
        pltpu.make_async_copy(
            held.at[chunk, array, block], held.at[chunk, array, block], ring_recv.at[chunk, array, block]
        ).wait()

    half = ys // 2

    def open_ring(chunk):
        for way in range(3):
            for array in range(2):
                pass_on(chunk, array, tp_me, way)

    def ring_step(chunk, distance):
        last = distance == half
        for array in range(2):
            for way in range(2):
                if last and array != way:
                    continue
                block = block_at(-distance if way == 0 else distance, core)
                arrive(chunk, array, block)
                if distance + 1 < half or (distance + 1 == half and array == way):
                    pass_on(chunk, array, block, way)
                pass_on(chunk, array, block, 2)

    def sibling_step(chunk, distance):
        for array in range(2):
            for way in range(2):
                if distance == 0 and way == 1 or distance == half and way != array:
                    continue
                arrive(chunk, array, block_at(-distance if way == 0 else distance, 1 - core))

    groups = ys // 2
    first = y_me // 2
    lean = 2 * lax.rem(y_me, 2) - 1
    group_order = [first] if groups == 1 else [first, first + lean, first - lean, first + 2]
    group_after = [1, 2, 3, 4]
    if groups == 2:
        group_order, group_after = [first, first + 1], [1, 2]
    if groups == 1:
        group_after = [1]
    depth = features // groups

    def multiply(chunk, place):
        group = lax.rem(group_order[place] + groups, groups)
        at = pl.ds(pl.multiple_of(group * depth, LANES), depth)
        pieces = pl.ds(group * (tp // groups), tp // groups)
        values = held[chunk, 0, pieces].reshape(depth, LANES).astype(jnp.float32)
        scaled = (values * gain_col[at, :]).astype(jnp.bfloat16)
        squares = jnp.sum(values * values, axis=0, keepdims=True)
        logit = jnp.sum(values * router_col[at, :], axis=0, keepdims=True)
        cotangent = held[chunk, 1, pieces].reshape(depth, LANES)
        gate = jnp.dot(gate_v[:, at], scaled, preferred_element_type=jnp.float32)
        up = jnp.dot(up_v[:, at], scaled, preferred_element_type=jnp.float32)
        back = jnp.dot(down_v[:, at], cotangent, preferred_element_type=jnp.float32)
        if place == 0:
            gate_sum[chunk] = gate
            up_sum[chunk] = up
            back_sum[chunk] = back
        else:
            gate_sum[chunk] += gate
            up_sum[chunk] += up
            back_sum[chunk] += back
        return squares, logit

    def share_dots(chunk):
        copies = []
        for step in range(1, tp):
            copy = pltpu.make_async_remote_copy(
                src_ref=dots.at[chunk, tp_me],
                dst_ref=dots.at[chunk, tp_me],
                send_sem=dot_send.at[chunk, step],
                recv_sem=dot_recv.at[chunk, tp_me],
                device_id={"tp": lax.rem(tp_me + step, tp)},
                device_id_type=MESH,
            )
            copy.start()
            sent.append(copy)

    def await_dots(chunk):
        for step in range(1, tp):
            peer = lax.rem(tp_me + step, tp)
            pltpu.make_async_copy(dots.at[chunk, peer], dots.at[chunk, peer], dot_recv.at[chunk, peer]).wait()

    def finish(chunk, squares, logit):
        inverse = lax.rsqrt(squares / features + EPSILON)
        prob = 1.0 / (1.0 + jnp.exp(-logit))
        gate = gate_sum[chunk] * inverse
        up = up_sum[chunk] * inverse
        back = back_sum[chunk]
        square = gate * gate
        bend = jnp.tanh(ROOT * gate * (1.0 + CUBIC * square))
        plus = 0.5 * (1.0 + bend)
        slope = plus + 0.5 * gate * (1.0 - bend * bend) * (ROOT * (1.0 + (3.0 * CUBIC) * square))
        act = gate * plus
        h_back = act * up * back
        dots[chunk, tp_me] = jnp.sum(h_back, axis=0, keepdims=True)
        share_dots(chunk)
        term = gate * up * slope * back * prob
        if chunk == 0:
            unit_sum[0] = term
            unit_sum[1] = h_back * prob
        else:
            unit_sum[0] += term
            unit_sum[1] += h_back * prob
        return prob

    open_ring(0)
    for chunk in range(1, chunks):
        select(chunk)
        open_ring(chunk)
    relay(0)
    loads[3].wait()
    loads[4].wait()
    gain = gain_v[...].astype(jnp.float32)
    for i in range(features // LANES):
        at = slice(i * LANES, (i + 1) * LANES)
        gain_col[at, :] = column(gain[at].reshape(1, LANES))
        router_col[at, :] = column(router_v[at].reshape(1, LANES))
    for load in loads[5:]:
        load.wait()

    probs = []
    totals = [None] * chunks
    for chunk in range(chunks):
        sibling_step(chunk, 0)
    done = 0
    for distance in range(1, half + 1):
        for chunk in range(chunks):
            ring_step(chunk, distance)
        relay(distance)
        ready = done < len(group_after) and group_after[done] <= distance
        for chunk in range(chunks):
            sibling_step(chunk, distance)
            if ready:
                more = multiply(chunk, done)
                totals[chunk] = more if done == 0 else (totals[chunk][0] + more[0], totals[chunk][1] + more[1])
            if distance == half:
                probs.append(finish(chunk, *totals[chunk]))
        done += int(ready)

    def share(buffer, send, recv, mine, count_of, peer_of):
        for step in range(1, count_of):
            copy = pltpu.make_async_remote_copy(
                src_ref=buffer.at[mine],
                dst_ref=buffer.at[mine],
                send_sem=send.at[step],
                recv_sem=recv.at[mine],
                device_id={"seq": peer_of(lax.rem(mine + step, count_of))},
                device_id_type=MESH,
            )
            copy.start()
            sent.append(copy)

    def collect(buffer, recv, mine, count_of):
        for step in range(1, count_of):
            peer = lax.rem(mine + step, count_of)
            pltpu.make_async_copy(buffer.at[peer], buffer.at[peer], recv.at[peer]).wait()
        total = buffer[0]
        for i in range(1, count_of):
            total = total + buffer[i]
        return total

    for i in range(half + 1, rounds):
        relay(i)
    if rounds > 0:
        relay_wait(rounds - 1)

    for i in range(2):
        unit_x[x_me, i : i + 1, :] = jnp.sum(jnp.transpose(unit_sum[i]), axis=0, keepdims=True)
    share(unit_x, ux_send, ux_recv, x_me, xs, along_x)

    weighted = None
    for chunk in range(chunks):
        await_dots(chunk)
        total = dots[chunk, 0]
        for i in range(1, tp):
            total = total + dots[chunk, i]
        coef = probs[chunk] * (1.0 - probs[chunk]) * total
        more = held[chunk, 0, tp_me].astype(jnp.float32) * coef
        weighted = more if weighted is None else weighted + more
    weighted = weighted * router_col[pl.ds(pl.multiple_of(tp_me * width, 8), width), :]
    score_x[x_me] = jnp.sum(jnp.transpose(weighted), axis=0, keepdims=True)
    share(score_x, sx_send, sx_recv, x_me, xs, along_x)

    unit_z[z_me] = collect(unit_x, ux_recv, x_me, xs)
    share(unit_z, uz_send, uz_recv, z_me, zs, along_z)
    score_z[z_me] = collect(score_x, sx_recv, x_me, xs)
    share(score_z, sz_send, sz_recv, z_me, zs, along_z)

    unit = collect(unit_z, uz_recv, z_me, zs) * factor
    unit_ref[0:2, :] = unit
    unit_ref[2:3, :] = unit[1:2, :]
    score_ref[...] = collect(score_z, sz_recv, z_me, zs) * factor
    for copy in sent:
        copy.wait_send()


def body(sizes, hidden, grad_out, router_w, norm_gain, gate_w, up_w, down_w, counts, order):
    xs, zs, ys, chunks, factor = sizes
    tp = ys * CORES
    tokens, width = hidden.shape
    features, units = gate_w.shape
    dma = pltpu.SemaphoreType.DMA
    f32, bf16 = jnp.float32, jnp.bfloat16
    anywhere = pl.BlockSpec(memory_space=pl.ANY)
    in_vmem = pl.BlockSpec(memory_space=pltpu.VMEM)
    unit, score = pl.pallas_call(
        functools.partial(kernel, sizes),
        out_shape=(jax.ShapeDtypeStruct((3, units), f32), jax.ShapeDtypeStruct((1, width), f32)),
        in_specs=[
            anywhere, anywhere, anywhere, anywhere, anywhere, anywhere, anywhere,
            pl.BlockSpec(memory_space=pltpu.SMEM), anywhere,
        ],
        out_specs=(in_vmem, in_vmem),
        scratch_shapes=[
            pltpu.VMEM((width, tokens), bf16),
            pltpu.VMEM((width, tokens), bf16),
            pltpu.VMEM((units, features), bf16),
            pltpu.VMEM((units, features), bf16),
            pltpu.VMEM((units, features), bf16),
            pltpu.VMEM((features,), f32),
            pltpu.VMEM((features,), bf16),
            pltpu.VMEM((1, order.shape[1]), jnp.int32),
            pltpu.VMEM((chunks, 2, tp, width, LANES), bf16),
            pltpu.VMEM((features, LANES), f32),
            pltpu.VMEM((features, LANES), f32),
            pltpu.VMEM((chunks, units, LANES), f32),
            pltpu.VMEM((chunks, units, LANES), f32),
            pltpu.VMEM((chunks, units, LANES), f32),
            pltpu.VMEM((2, units, LANES), f32),
            pltpu.VMEM((chunks, tp, 1, LANES), f32),
            pltpu.VMEM((xs, 2, units), f32),
            pltpu.VMEM((zs, 2, units), f32),
            pltpu.VMEM((xs, 1, width), f32),
            pltpu.VMEM((zs, 1, width), f32),
            dma((8,)),
            pltpu.SemaphoreType.REGULAR((8,)),
            dma((chunks, 2, tp, 3)),
            dma((chunks, 2, tp)),
            dma((chunks, tp)),
            dma((chunks, tp)),
            dma((xs,)),
            dma((xs,)),
            dma((zs,)),
            dma((zs,)),
            dma((xs,)),
            dma((xs,)),
            dma((zs,)),
            dma((zs,)),
        ],
        compiler_params=pltpu.CompilerParams(
            collective_id=0, has_side_effects=True, vmem_limit_bytes=62 * 1024 * 1024
        ),
    )(
        hidden.T,
        grad_out.T,
        router_w,
        norm_gain,
        gate_w.T,
        up_w.T,
        down_w,
        counts,
        order,
    )
    return unit, score.reshape(width)


def solution(mesh):
    seq, tp = mesh.shape["seq"], mesh.shape["tp"]
    xs = X_CHIPS if seq % X_CHIPS == 0 else 1
    chunks = 3
    sizes = (xs, seq // xs, tp // CORES, chunks, float(LANES * seq) ** -0.5)
    in_specs = (
        P("seq", "tp"),
        P("seq", "tp"),
        P(),
        P(),
        P(None, "tp"),
        P(None, "tp"),
        P("tp", None),
        P("seq"),
        P("seq", None),
    )
    return jax.shard_map(
        functools.partial(body, sizes),
        mesh=mesh,
        in_specs=in_specs,
        out_specs=(P(None, "tp"), P("tp")),
        check_vma=False,
    )
```

time: 276 us -> 71.1 us (0.26)
  the two profiles are of different devices: /device:TPU:32 before, /device:TPU:1 now
where the time goes in v1:
time: 71.1 us; the launch traced here: 70.9 us
  Pallas kernels  67.1 us (94%)
  local copies, waits for them, and re-layouts  2.51 us (4%)
  between operations  1.29 us (2%)
    pallas_call x1, Pallas kernels, body(): pl.pallas_call(functools.partial(kernel, sizes), out_shape=(jax.ShapeDtyp...  67.1 us
    unnamed x2, local copies, waits for them, and re-layouts  2.51 us

profile of v1, /device:TPU:1, one launch (start us, length us, event | category | flops | bytes accessed | tf_op | source)
XLA Modules:
  0.0 70.9 jit_solution(1373236443927963354)
XLA Ops:
  1.3 67.1 %shard_map.104 = (f32[3,448]{1,0:T(4,128)}, f32[1,224]{1,0:T(1,128)}) custom-call(bf16[224,1024]{1,0:T(8,128)(2,1)} %bitcast.7, bf16[224,1024]{1,0:T(8,128)(2,1)} %bitcast.8, f32[3584]{0:T(1024)} %router_hbm.1, bf16[3584]{0:T(1024)(128)(2,1)} %gain_hbm.1, bf16[448,3584]{1,0:T(8,128)(2,1)} %bitcast.5, bf16[448,3584]{1,0:T(8,128)(2,1)} %bitcast.6, ...), custom_call_target="tpu_custom_call" | custom-call | tf_op jit(solution)/shard_map/pallas_call | solution.py:329
  68.4 1.3 %copy.14 = f32[3,448]{1,0:T(4,128)} copy(f32[3,448]{1,0:T(4,128)} %get-tuple-element.8) | data formatting | bytes 10752
  69.7 1.2 %copy.15 = f32[224]{0:T(256)} copy(f32[224]{0:T(256)} %bitcast.9) | data formatting | bytes 1792

commit v2 on v1

v2 whole, which is shorter than its diff:
```python
import functools

import jax
import jax.numpy as jnp
from jax import lax
from jax.experimental import pallas as pl
from jax.experimental.pallas import tpu as pltpu
from jax.sharding import PartitionSpec as P

MESH = pl.DeviceIdType.MESH
LANES = 128
CORES = 2
X_CHIPS = 4
EPSILON = 1e-06
ROOT = 0.7978845608028654
CUBIC = 0.044715


def column(row):
    return jnp.transpose(jnp.broadcast_to(row, (LANES, LANES)))


def kernel(
    sizes,
    hidden_hbm, grad_hbm, router_hbm, gain_hbm, gate_hbm, up_hbm, down_hbm, counts_hbm, order_hbm,
    unit_ref, score_ref,
    hidden_v, grad_v, gate_v, up_v, down_v, router_v, gain_v, order_v, count_v, held, gain_col, router_col,
    gate_sum, up_sum, back_sum, unit_sum, dots, unit_x, unit_z, score_all,
    load_sem, near_sem, ring_send, ring_recv, dot_send, dot_recv, ux_send, ux_recv, uz_send, uz_recv,
    score_send, score_recv,
):
    xs, zs, ys, chunks, factor = sizes
    tp = ys * CORES
    width = hidden_v.shape[0]
    tokens = hidden_v.shape[1]
    features = width * tp
    seq_me = lax.axis_index("seq")
    tp_me = lax.axis_index("tp")
    x_me, z_me = lax.rem(seq_me, xs), seq_me // xs
    y_me, core = tp_me // CORES, lax.rem(tp_me, CORES)
    sibling = y_me * CORES + (1 - core)

    def block_at(distance, of_core):
        return lax.rem(y_me + distance + ys, ys) * CORES + of_core

    right, left = block_at(1, core), block_at(-1, core)

    loads = [
        pltpu.make_async_copy(source, target, load_sem.at[i])
        for i, (source, target) in enumerate(
            [
                (order_hbm, order_v), (counts_hbm, count_v), (hidden_hbm, hidden_v), (grad_hbm, grad_v),
                (router_hbm, router_v), (gain_hbm, gain_v), (gate_hbm, gate_v), (up_hbm, up_v), (down_hbm, down_v),
            ]
        )
    ]
    for load in loads[:4]:
        load.start()

    barrier = pltpu.get_barrier_semaphore()
    along_x = lambda i: z_me * xs + lax.rem(i + xs, xs)
    along_z = lambda i: lax.rem(i + zs, zs) * xs + x_me
    beside_x = [along_x(x_me + i) for i in ((1, -1) if xs > 2 else (1,) if xs > 1 else ())]
    beside_z = [along_z(z_me + i) for i in ((1, -1) if zs > 2 else (1,) if zs > 1 else ())]
    beside_y = [right, left] if ys > 2 else [right]
    for peer in beside_y + [sibling]:
        pl.semaphore_signal(barrier, inc=1, device_id={"tp": peer}, device_id_type=MESH)
    for peer in beside_x + beside_z:
        pl.semaphore_signal(barrier, inc=1, device_id={"seq": peer}, device_id_type=MESH)

    rounds = zs // 2 + xs // 2 - 1
    relayed = []

    def relay():
        i = len(relayed)
        if i > rounds:
            return
        relayed.append(i)
        if i > 0:
            pl.semaphore_wait(near_sem.at[i - 1], len(beside_x + beside_z))
        if i < rounds:
            for peer in beside_x + beside_z:
                pl.semaphore_signal(near_sem.at[i], inc=1, device_id={"seq": peer}, device_id_type=MESH)

    token = lax.broadcasted_iota(jnp.int32, (tokens, LANES), 0)
    slot = lax.broadcasted_iota(jnp.int32, (1, LANES), 1)
    loads[0].wait()
    loads[1].wait()
    count = count_v[0]

    def choose(chunk):
        wanted = order_v[:, chunk * LANES : (chunk + 1) * LANES]
        wanted = jnp.where(slot + chunk * LANES < count, wanted, -1)
        return jnp.where(token == wanted, 1.0, 0.0).astype(jnp.bfloat16)

    def pick(chunk, array, chosen):
        rows = jnp.dot((hidden_v, grad_v)[array][...], chosen, preferred_element_type=jnp.float32)
        held[chunk, array, tp_me] = rows.astype(jnp.bfloat16)

    ring_sent = [0] * chunks

    def pass_on(chunk, array, block, way):
        target = (right, left, sibling)[way]
        copy = pltpu.make_async_remote_copy(
            src_ref=held.at[chunk, array, block],
            dst_ref=held.at[chunk, array, block],
            send_sem=ring_send.at[chunk],
            recv_sem=ring_recv.at[chunk, array, block],
            device_id={"tp": target},
            device_id_type=MESH,
        )
        copy.start()
        ring_sent[chunk] += 1

    def await_bytes(view, semaphore):
        pltpu.make_async_copy(view, view, semaphore).wait()

    def arrive(chunk, array, block):
        pltpu.make_async_copy(
            held.at[chunk, array, block], held.at[chunk, array, block], ring_recv.at[chunk, array, block]
        ).wait()

    half = ys // 2

    def open_ring(chunk):
        chosen = choose(chunk)
        for array in range(2):
            if chunk == 0:
                loads[2 + array].wait()
            pick(chunk, array, chosen)
            if chunk == 0 and array == 0:
                pl.semaphore_wait(barrier, len(beside_y) + 1 + len(beside_x) + len(beside_z))
            for way in range(2):
                if half > 1 or way == array:
                    pass_on(chunk, array, tp_me, way)

    def ring_step(chunk, distance):
        last = distance == half
        for array in range(2):
            for way in range(2):
                if last and array != way:
                    continue
                block = block_at(-distance if way == 0 else distance, core)
                arrive(chunk, array, block)
                if distance + 1 < half or (distance + 1 == half and array == way):
                    pass_on(chunk, array, block, way)
                pass_on(chunk, array, block, 2)

    def sibling_step(chunk, distance):
        for array in range(2):
            for way in range(2):
                if distance == 0 and way == 1 or distance == half and way != array:
                    continue
                arrive(chunk, array, block_at(-distance if way == 0 else distance, 1 - core))

    groups = ys // 2
    first = y_me // 2
    lean = 2 * lax.rem(y_me, 2) - 1
    group_order = [first] if groups == 1 else [first, first + lean, first - lean, first + 2]
    group_after = [1, 2, 3, 4]
    if groups == 2:
        group_order, group_after = [first, first + 1], [1, 2]
    if groups == 1:
        group_after = [1]
    depth = features // groups

    def multiply(chunk, place):
        group = lax.rem(group_order[place] + groups, groups)
        at = pl.ds(pl.multiple_of(group * depth, LANES), depth)
        pieces = pl.ds(group * (tp // groups), tp // groups)
        values = held[chunk, 0, pieces].reshape(depth, LANES).astype(jnp.float32)
        scaled = (values * gain_col[at, :]).astype(jnp.bfloat16)
        squares = jnp.sum(values * values, axis=0, keepdims=True)
        logit = jnp.sum(values * router_col[at, :], axis=0, keepdims=True)
        cotangent = held[chunk, 1, pieces].reshape(depth, LANES)
        gate = jnp.dot(gate_v[:, at], scaled, preferred_element_type=jnp.float32)
        up = jnp.dot(up_v[:, at], scaled, preferred_element_type=jnp.float32)
        back = jnp.dot(down_v[:, at], cotangent, preferred_element_type=jnp.float32)
        if place == 0:
            gate_sum[chunk] = gate
            up_sum[chunk] = up
            back_sum[chunk] = back
        else:
            gate_sum[chunk] += gate
            up_sum[chunk] += up
            back_sum[chunk] += back
        return squares, logit

    def far_first(count_of, gap):
        return sorted(range(1, count_of), key=lambda step: -min(step // gap, (count_of - step) // gap))

    def share_dots():
        for step in far_first(tp, CORES):
            copy = pltpu.make_async_remote_copy(
                src_ref=dots.at[tp_me],
                dst_ref=dots.at[tp_me],
                send_sem=dot_send.at[0],
                recv_sem=dot_recv.at[0],
                device_id={"tp": lax.rem(tp_me + step, tp)},
                device_id_type=MESH,
            )
            copy.start()

    def finish(chunk, squares, logit):
        inverse = lax.rsqrt(squares / features + EPSILON)
        prob = 1.0 / (1.0 + jnp.exp(-logit))
        gate = gate_sum[chunk] * inverse
        up = up_sum[chunk] * inverse
        back = back_sum[chunk]
        square = gate * gate
        bend = jnp.tanh(ROOT * gate * (1.0 + CUBIC * square))
        plus = 0.5 * (1.0 + bend)
        slope = plus + 0.5 * gate * (1.0 - bend * bend) * (ROOT * (1.0 + (3.0 * CUBIC) * square))
        act = gate * plus
        h_back = act * up * back
        dots[tp_me, chunk : chunk + 1, :] = jnp.sum(h_back, axis=0, keepdims=True)
        term = gate * up * slope * back * prob
        if chunk == 0:
            unit_sum[0] = term
            unit_sum[1] = h_back * prob
        else:
            unit_sum[0] += term
            unit_sum[1] += h_back * prob
        return prob

    for chunk in range(chunks):
        open_ring(chunk)
        if chunk == 0:
            relay()
            for load in loads[4:]:
                load.start()
    relay()
    for chunk in range(chunks):
        for array in range(2):
            pass_on(chunk, array, tp_me, 2)
    loads[4].wait()
    loads[5].wait()
    gain = gain_v[...].astype(jnp.float32)
    for i in range(features // LANES):
        at = slice(i * LANES, (i + 1) * LANES)
        gain_col[at, :] = column(gain[at].reshape(1, LANES))
        router_col[at, :] = column(router_v[at].reshape(1, LANES))
    for load in loads[6:]:
        load.wait()

    probs = [None] * chunks
    totals = [None] * chunks

    def compute(chunk, place):
        sibling_step(chunk, group_after[place])
        more = multiply(chunk, place)
        totals[chunk] = more if place == 0 else (totals[chunk][0] + more[0], totals[chunk][1] + more[1])
        if place == len(group_after) - 1:
            probs[chunk] = finish(chunk, *totals[chunk])

    for chunk in range(chunks):
        sibling_step(chunk, 0)
    waiting = []
    for distance in range(1, half + 1):
        for chunk in range(chunks):
            ring_step(chunk, distance)
            if waiting:
                compute(*waiting.pop(0))
            if distance in group_after:
                waiting.append((chunk, group_after.index(distance)))
            relay()
    for item in waiting:
        compute(*item)
    share_dots()

    def share(buffer, send, recv, mine, count_of, peer_of):
        for step in far_first(count_of, 1):
            copy = pltpu.make_async_remote_copy(
                src_ref=buffer.at[mine],
                dst_ref=buffer.at[mine],
                send_sem=send.at[0],
                recv_sem=recv.at[0],
                device_id={"seq": peer_of(lax.rem(mine + step, count_of))},
                device_id_type=MESH,
            )
            copy.start()

    def sent(buffer, send, count_of):
        if count_of > 1:
            await_bytes(buffer.at[pl.ds(0, count_of - 1)], send.at[0])

    def collect(buffer, recv, count_of):
        if count_of > 1:
            await_bytes(buffer.at[pl.ds(0, count_of - 1)], recv.at[0])
        total = buffer[0]
        for i in range(1, count_of):
            total = total + buffer[i]
        return total

    while len(relayed) <= rounds:
        relay()

    for i in range(2):
        unit_x[x_me, i : i + 1, :] = jnp.sum(jnp.transpose(unit_sum[i]), axis=0, keepdims=True)
    share(unit_x, ux_send, ux_recv, x_me, xs, along_x)
    for chunk in range(chunks):
        assert ring_sent[chunk] == 2 * (tp - 1)
        await_bytes(held.at[chunk, :, pl.ds(0, tp - 1)], ring_send.at[chunk])

    await_bytes(dots.at[pl.ds(0, tp - 1)], dot_recv.at[0])
    total = dots[0]
    for i in range(1, tp):
        total = total + dots[i]
    weighted = None
    for chunk in range(chunks):
        coef = probs[chunk] * (1.0 - probs[chunk]) * total[chunk : chunk + 1, :]
        more = held[chunk, 0, tp_me].astype(jnp.float32) * coef
        weighted = more if weighted is None else weighted + more
    weighted = weighted * router_col[pl.ds(pl.multiple_of(tp_me * width, 8), width), :]
    score_all[seq_me] = jnp.sum(jnp.transpose(weighted), axis=0, keepdims=True)
    ways = [(i, j) for i in range(zs) for j in range(xs) if i + j]
    for i, j in sorted(ways, key=lambda way: -min(way[0], zs - way[0]) - min(way[1], xs - way[1])):
        copy = pltpu.make_async_remote_copy(
            src_ref=score_all.at[seq_me],
            dst_ref=score_all.at[seq_me],
            send_sem=score_send.at[0],
            recv_sem=score_recv.at[0],
            device_id={"seq": lax.rem(z_me + i, zs) * xs + lax.rem(x_me + j, xs)},
            device_id_type=MESH,
        )
        copy.start()

    unit_z[z_me] = collect(unit_x, ux_recv, xs)
    share(unit_z, uz_send, uz_recv, z_me, zs, along_z)
    await_bytes(dots.at[pl.ds(0, tp - 1)], dot_send.at[0])
    sent(unit_x, ux_send, xs)

    unit = collect(unit_z, uz_recv, zs) * factor
    unit_ref[0:2, :] = unit
    unit_ref[2:3, :] = unit[1:2, :]
    sent(unit_z, uz_send, zs)
    score_ref[...] = collect(score_all, score_recv, xs * zs) * factor
    sent(score_all, score_send, xs * zs)


def body(sizes, hidden, grad_out, router_w, norm_gain, gate_w, up_w, down_w, counts, order):
    xs, zs, ys, chunks, factor = sizes
    tp = ys * CORES
    tokens, width = hidden.shape
    features, units = gate_w.shape
    dma = pltpu.SemaphoreType.DMA
    f32, bf16 = jnp.float32, jnp.bfloat16
    in_hbm = pl.BlockSpec(memory_space=pl.ANY)
    in_vmem = pl.BlockSpec(memory_space=pltpu.VMEM)
    unit, score = pl.pallas_call(
        functools.partial(kernel, sizes),
        out_shape=(jax.ShapeDtypeStruct((3, units), f32), jax.ShapeDtypeStruct((1, width), f32)),
        in_specs=[
            in_hbm, in_hbm, in_hbm, in_hbm, in_hbm, in_hbm, in_hbm, in_hbm, in_hbm,
        ],
        out_specs=(in_vmem, in_vmem),
        scratch_shapes=[
            pltpu.VMEM((width, tokens), bf16),
            pltpu.VMEM((width, tokens), bf16),
            pltpu.VMEM((units, features), bf16),
            pltpu.VMEM((units, features), bf16),
            pltpu.VMEM((units, features), bf16),
            pltpu.VMEM((features,), f32),
            pltpu.VMEM((features,), bf16),
            pltpu.VMEM((1, order.shape[1]), jnp.int32),
            pltpu.SMEM((1,), jnp.int32),
            pltpu.VMEM((chunks, 2, tp, width, LANES), bf16),
            pltpu.VMEM((features, LANES), f32),
            pltpu.VMEM((features, LANES), f32),
            pltpu.VMEM((chunks, units, LANES), f32),
            pltpu.VMEM((chunks, units, LANES), f32),
            pltpu.VMEM((chunks, units, LANES), f32),
            pltpu.VMEM((2, units, LANES), f32),
            pltpu.VMEM((tp, chunks, LANES), f32),
            pltpu.VMEM((xs, 2, units), f32),
            pltpu.VMEM((zs, 2, units), f32),
            pltpu.VMEM((xs * zs, 1, width), f32),
            dma((9,)),
            pltpu.SemaphoreType.REGULAR((8,)),
            dma((chunks,)),
            dma((chunks, 2, tp)),
            dma((1,)),
            dma((1,)),
            dma((1,)),
            dma((1,)),
            dma((1,)),
            dma((1,)),
            dma((1,)),
            dma((1,)),
        ],
        compiler_params=pltpu.CompilerParams(
            collective_id=0, has_side_effects=True, vmem_limit_bytes=62 * 1024 * 1024
        ),
    )(
        hidden.T,
        grad_out.T,
        router_w,
        norm_gain,
        gate_w.T,
        up_w.T,
        down_w,
        counts,
        order,
    )
    return unit, score.reshape(width)


def solution(mesh):
    seq, tp = mesh.shape["seq"], mesh.shape["tp"]
    xs = X_CHIPS if seq % X_CHIPS == 0 else 1
    chunks = 3
    sizes = (xs, seq // xs, tp // CORES, chunks, float(LANES * seq) ** -0.5)
    in_specs = (
        P("seq", "tp"),
        P("seq", "tp"),
        P(),
        P(),
        P(None, "tp"),
        P(None, "tp"),
        P("tp", None),
        P("seq"),
        P("seq", None),
    )
    return jax.shard_map(
        functools.partial(body, sizes),
        mesh=mesh,
        in_specs=in_specs,
        out_specs=(P(None, "tp"), P("tp")),
        check_vma=False,
    )
```

time: 71.1 us -> 64.6 us (0.909)
  Pallas kernels: 67.1 us -> 60.6 us
    pallas_call x1, Pallas kernels: 67.1 us -> 60.6 us  [body(): pl.pallas_call(functools.partial(kernel, sizes), out_shape=(jax.ShapeDtyp...]
where the time goes in v2:
time: 64.6 us; the launch traced here: 64.4 us
  Pallas kernels  60.6 us (94%)
  local copies, waits for them, and re-layouts  2.51 us (4%)
  between operations  1.29 us (2%)
    pallas_call x1, Pallas kernels, body(): pl.pallas_call(functools.partial(kernel, sizes), out_shape=(jax.ShapeDtyp...  60.6 us
    unnamed x2, local copies, waits for them, and re-layouts  2.51 us

profile of v2, /device:TPU:1, one launch (start us, length us, event | category | flops | bytes accessed | tf_op | source)
XLA Modules:
  0.0 64.4 jit_solution(7225884956405402630)
XLA Ops:
  1.3 60.6 %shard_map.104 = (f32[3,448]{1,0:T(4,128)}, f32[1,224]{1,0:T(1,128)}) custom-call(bf16[224,1024]{1,0:T(8,128)(2,1)} %bitcast.7, bf16[224,1024]{1,0:T(8,128)(2,1)} %bitcast.8, f32[3584]{0:T(1024)} %router_hbm.1, bf16[3584]{0:T(1024)(128)(2,1)} %gain_hbm.1, bf16[448,3584]{1,0:T(8,128)(2,1)} %bitcast.5, bf16[448,3584]{1,0:T(8,128)(2,1)} %bitcast.6, ...), custom_call_target="tpu_custom_call" | custom-call | tf_op jit(solution)/shard_map/pallas_call | solution.py:350
  61.9 1.3 %copy.14 = f32[3,448]{1,0:T(4,128)} copy(f32[3,448]{1,0:T(4,128)} %get-tuple-element.8) | data formatting | bytes 10752
  63.2 1.2 %copy.15 = f32[224]{0:T(256)} copy(f32[224]{0:T(256)} %bitcast.9) | data formatting | bytes 1792

commit v3 on v2

--- a/solution.py
+++ b/solution.py
@@ -330,12 +330,17 @@
     await_bytes(dots.at[pl.ds(0, tp - 1)], dot_send.at[0])
     sent(unit_x, ux_send, xs)
 
-    unit = collect(unit_z, uz_recv, zs) * factor
-    unit_ref[0:2, :] = unit
-    unit_ref[2:3, :] = unit[1:2, :]
+    unit_ref[...] = collect(unit_z, uz_recv, zs)
     sent(unit_z, uz_send, zs)
-    score_ref[...] = collect(score_all, score_recv, xs * zs) * factor
+    score_ref[...] = collect(score_all, score_recv, xs * zs)
     sent(score_all, score_send, xs * zs)
+
+
+def scale(factor, unit_ref, score_ref, unit_out, score_out):
+    unit = unit_ref[...] * factor
+    unit_out[0:2, :] = unit
+    unit_out[2:3, :] = unit[1:2, :]
+    score_out[...] = score_ref[...] * factor
 
 
 def body(sizes, hidden, grad_out, router_w, norm_gain, gate_w, up_w, down_w, counts, order):
@@ -349,7 +354,7 @@
     in_vmem = pl.BlockSpec(memory_space=pltpu.VMEM)
     unit, score = pl.pallas_call(
         functools.partial(kernel, sizes),
-        out_shape=(jax.ShapeDtypeStruct((3, units), f32), jax.ShapeDtypeStruct((1, width), f32)),
+        out_shape=(jax.ShapeDtypeStruct((2, units), f32), jax.ShapeDtypeStruct((1, width), f32)),
         in_specs=[
             in_hbm, in_hbm, in_hbm, in_hbm, in_hbm, in_hbm, in_hbm, in_hbm, in_hbm,
         ],
@@ -402,6 +407,12 @@
         counts,
         order,
     )
+    unit, score = pl.pallas_call(
+        functools.partial(scale, factor),
+        out_shape=(jax.ShapeDtypeStruct((3, units), f32), jax.ShapeDtypeStruct((1, width), f32)),
+        in_specs=[in_vmem, in_vmem],
+        out_specs=(in_vmem, in_vmem),
+    )(unit, score)
     return unit, score.reshape(width)
 
 

time: 64.6 us -> 63.4 us (0.981)
  local copies, waits for them, and re-layouts: 2.51 us -> 0 us
  Pallas kernels: 60.6 us -> 61.9 us
    unnamed x2 -> x0, local copies, waits for them, and re-layouts: 2.51 us -> none
    pallas_call x0 -> x1, Pallas kernels: none -> 1.28 us  [body(): pl.pallas_call(functools.partial(scale, factor), out_shape=(jax.ShapeDtyp...]
where the time goes in v3:
time: 63.4 us; the launch traced here: 63.2 us
  Pallas kernels  61.9 us (98%)
  between operations  1.29 us (2%)
    pallas_call x1, Pallas kernels, body(): pl.pallas_call(functools.partial(kernel, sizes), out_shape=(jax.ShapeDtyp...  60.6 us
    pallas_call x1, Pallas kernels, body(): pl.pallas_call(functools.partial(scale, factor), out_shape=(jax.ShapeDtyp...  1.28 us

profile of v3, /device:TPU:1, one launch (start us, length us, event | category | flops | bytes accessed | tf_op | source)
XLA Modules:
  0.0 63.2 jit_solution(3164212663911439868)
XLA Ops:
  1.3 60.6 %shard_map.104 = (f32[2,448]{1,0:T(2,128)}, f32[1,224]{1,0:T(1,128)}) custom-call(bf16[224,1024]{1,0:T(8,128)(2,1)} %bitcast.7, bf16[224,1024]{1,0:T(8,128)(2,1)} %bitcast.8, f32[3584]{0:T(1024)} %router_hbm.1, bf16[3584]{0:T(1024)(128)(2,1)} %gain_hbm.1, bf16[448,3584]{1,0:T(8,128)(2,1)} %bitcast.5, bf16[448,3584]{1,0:T(8,128)(2,1)} %bitcast.6, ...), custom_call_target="tpu_custom_call" | custom-call | tf_op jit(solution)/shard_map/pallas_call | solution.py:355
  61.9 1.3 %shard_map.105 = (f32[3,448]{1,0:T(4,128)}, f32[1,224]{1,0:T(1,128)}) custom-call(f32[2,448]{1,0:T(2,128)} %get-tuple-element.6.unit_ref, f32[1,224]{1,0:T(1,128)} %get-tuple-element.7.score_ref), custom_call_target="tpu_custom_call" | custom-call | tf_op jit(solution)/shard_map/pallas_call | solution.py:410

commit v4 on v3

--- a/solution.py
+++ b/solution.py
@@ -136,6 +136,7 @@
 
     def ring_step(chunk, distance):
         last = distance == half
+        across = []
         for array in range(2):
             for way in range(2):
                 if last and array != way:
@@ -144,7 +145,9 @@
                 arrive(chunk, array, block)
                 if distance + 1 < half or (distance + 1 == half and array == way):
                     pass_on(chunk, array, block, way)
-                pass_on(chunk, array, block, 2)
+                across.append((array, block))
+        for array, block in across:
+            pass_on(chunk, array, block, 2)
 
     def sibling_step(chunk, distance):
         for array in range(2):
@@ -164,27 +167,29 @@
         group_after = [1]
     depth = features // groups
 
-    def multiply(chunk, place):
+    def multiply(picked, place):
         group = lax.rem(group_order[place] + groups, groups)
         at = pl.ds(pl.multiple_of(group * depth, LANES), depth)
         pieces = pl.ds(group * (tp // groups), tp // groups)
-        values = held[chunk, 0, pieces].reshape(depth, LANES).astype(jnp.float32)
-        scaled = (values * gain_col[at, :]).astype(jnp.bfloat16)
-        squares = jnp.sum(values * values, axis=0, keepdims=True)
-        logit = jnp.sum(values * router_col[at, :], axis=0, keepdims=True)
-        cotangent = held[chunk, 1, pieces].reshape(depth, LANES)
-        gate = jnp.dot(gate_v[:, at], scaled, preferred_element_type=jnp.float32)
-        up = jnp.dot(up_v[:, at], scaled, preferred_element_type=jnp.float32)
-        back = jnp.dot(down_v[:, at], cotangent, preferred_element_type=jnp.float32)
-        if place == 0:
-            gate_sum[chunk] = gate
-            up_sum[chunk] = up
-            back_sum[chunk] = back
-        else:
-            gate_sum[chunk] += gate
-            up_sum[chunk] += up
-            back_sum[chunk] += back
-        return squares, logit
+        scaled, cotangent, sums = [], [], []
+        for chunk in picked:
+            values = held[chunk, 0, pieces].reshape(depth, LANES).astype(jnp.float32)
+            scaled.append((values * gain_col[at, :]).astype(jnp.bfloat16))
+            cotangent.append(held[chunk, 1, pieces].reshape(depth, LANES))
+            squares = jnp.sum(values * values, axis=0, keepdims=True)
+            logit = jnp.sum(values * router_col[at, :], axis=0, keepdims=True)
+            sums.append((squares, logit))
+        scaled = jnp.concatenate(scaled, axis=1)
+        cotangent = jnp.concatenate(cotangent, axis=1)
+        for total, weight, rows in ((gate_sum, gate_v, scaled), (up_sum, up_v, scaled), (back_sum, down_v, cotangent)):
+            product = jnp.dot(weight[:, at], rows, preferred_element_type=jnp.float32)
+            for i, chunk in enumerate(picked):
+                part = product[:, i * LANES : (i + 1) * LANES]
+                if place == 0:
+                    total[chunk] = part
+                else:
+                    total[chunk] += part
+        return sums
 
     def far_first(count_of, gap):
         return sorted(range(1, count_of), key=lambda step: -min(step // gap, (count_of - step) // gap))
@@ -246,12 +251,15 @@
     probs = [None] * chunks
     totals = [None] * chunks
 
-    def compute(chunk, place):
-        sibling_step(chunk, group_after[place])
-        more = multiply(chunk, place)
-        totals[chunk] = more if place == 0 else (totals[chunk][0] + more[0], totals[chunk][1] + more[1])
+    def compute(picked, place):
+        for chunk in picked:
+            sibling_step(chunk, group_after[place])
+        sums = multiply(picked, place)
+        for chunk, more in zip(picked, sums):
+            totals[chunk] = more if place == 0 else (totals[chunk][0] + more[0], totals[chunk][1] + more[1])
         if place == len(group_after) - 1:
-            probs[chunk] = finish(chunk, *totals[chunk])
+            for chunk in picked:
+                probs[chunk] = finish(chunk, *totals[chunk])
 
     for chunk in range(chunks):
         sibling_step(chunk, 0)
@@ -259,13 +267,13 @@
     for distance in range(1, half + 1):
         for chunk in range(chunks):
             ring_step(chunk, distance)
-            if waiting:
+            if waiting and not (distance == half and chunk == chunks - 1):
                 compute(*waiting.pop(0))
             if distance in group_after:
-                waiting.append((chunk, group_after.index(distance)))
+                waiting.append(([chunk], group_after.index(distance)))
             relay()
-    for item in waiting:
-        compute(*item)
+    if waiting:
+        compute([chunk for picked, _ in waiting for chunk in picked], waiting[0][1])
     share_dots()
 
     def share(buffer, send, recv, mine, count_of, peer_of):
@@ -302,16 +310,18 @@
         assert ring_sent[chunk] == 2 * (tp - 1)
         await_bytes(held.at[chunk, :, pl.ds(0, tp - 1)], ring_send.at[chunk])
 
+    share_of_router = router_col[pl.ds(pl.multiple_of(tp_me * width, 8), width), :]
+    terms = [
+        held[chunk, 0, tp_me].astype(jnp.float32) * share_of_router * (probs[chunk] * (1.0 - probs[chunk]))
+        for chunk in range(chunks)
+    ]
     await_bytes(dots.at[pl.ds(0, tp - 1)], dot_recv.at[0])
     total = dots[0]
     for i in range(1, tp):
         total = total + dots[i]
-    weighted = None
-    for chunk in range(chunks):
-        coef = probs[chunk] * (1.0 - probs[chunk]) * total[chunk : chunk + 1, :]
-        more = held[chunk, 0, tp_me].astype(jnp.float32) * coef
-        weighted = more if weighted is None else weighted + more
-    weighted = weighted * router_col[pl.ds(pl.multiple_of(tp_me * width, 8), width), :]
+    weighted = terms[0] * total[0:1, :]
+    for chunk in range(1, chunks):
+        weighted = weighted + terms[chunk] * total[chunk : chunk + 1, :]
     score_all[seq_me] = jnp.sum(jnp.transpose(weighted), axis=0, keepdims=True)
     ways = [(i, j) for i in range(zs) for j in range(xs) if i + j]
     for i, j in sorted(ways, key=lambda way: -min(way[0], zs - way[0]) - min(way[1], xs - way[1])):
@@ -412,6 +422,7 @@
         out_shape=(jax.ShapeDtypeStruct((3, units), f32), jax.ShapeDtypeStruct((1, width), f32)),
         in_specs=[in_vmem, in_vmem],
         out_specs=(in_vmem, in_vmem),
+        compiler_params=pltpu.CompilerParams(vmem_limit_bytes=62 * 1024 * 1024),
     )(unit, score)
     return unit, score.reshape(width)
 

time: 63.4 us -> 63.6 us (level)
  no operation moved by 1% of the time
where the time goes in v4:
time: 63.6 us; the launch traced here: 63.3 us
  Pallas kernels  62.1 us (98%)
  between operations  1.29 us (2%)
    pallas_call x1, Pallas kernels, body(): pl.pallas_call(functools.partial(kernel, sizes), out_shape=(jax.ShapeDtyp...  60.8 us
    pallas_call x1, Pallas kernels, body(): pl.pallas_call(functools.partial(scale, factor), out_shape=(jax.ShapeDtyp...  1.28 us

profile of v4, /device:TPU:1, one launch (start us, length us, event | category | flops | bytes accessed | tf_op | source)
XLA Modules:
  0.0 63.3 jit_solution(4168691931961490453)
XLA Ops:
  1.3 60.8 %shard_map.104 = (f32[2,448]{1,0:T(2,128)}, f32[1,224]{1,0:T(1,128)}) custom-call(bf16[224,1024]{1,0:T(8,128)(2,1)} %bitcast.7, bf16[224,1024]{1,0:T(8,128)(2,1)} %bitcast.8, f32[3584]{0:T(1024)} %router_hbm.1, bf16[3584]{0:T(1024)(128)(2,1)} %gain_hbm.1, bf16[448,3584]{1,0:T(8,128)(2,1)} %bitcast.5, bf16[448,3584]{1,0:T(8,128)(2,1)} %bitcast.6, ...), custom_call_target="tpu_custom_call" | custom-call | tf_op jit(solution)/shard_map/pallas_call | solution.py:365
  62.1 1.3 %shard_map.105 = (f32[3,448]{1,0:T(4,128)}, f32[1,224]{1,0:T(1,128)}) custom-call(f32[2,448]{1,0:T(2,128)} %get-tuple-element.6.unit_ref, f32[1,224]{1,0:T(1,128)} %get-tuple-element.7.score_ref), custom_call_target="tpu_custom_call" | custom-call | tf_op jit(solution)/shard_map/pallas_call | solution.py:420
